TPU v7x, 128 devices: a whole 4x4x4 slice. The times are simulated.
128 devices in a mesh: dp: 4 (over z), mp: 32 (over x, y, core).
Axes of the slice: x: 4, y: 4, z: 4, core: 2. Of those that a mesh axis runs over, the one named last changes fastest.
Arguments:
- tokens: bfloat16 [16384, 4096], P(('dp', 'mp')), may hold values from -6 to 6
- expert_ids: int32 [16384, 1], P(('dp', 'mp')), may hold values from 0 to 63; in each aligned block of 128 rows (0 to 127, 128 to 255, ...) at most 3 rows name the same one
- gate_probs: float32 [16384, 1], P(('dp', 'mp')), may hold values from 0.3 to 1
- gate_weight: bfloat16 [64, 4096, 1536], P('mp', None, 'dp'), may hold values from -0.09375 to 0.09375
- up_weight: bfloat16 [64, 4096, 1536], P('mp', None, 'dp'), may hold values from -0.09375 to 0.09375
- down_weight: bfloat16 [64, 1536, 4096], P('mp', 'dp'), may hold values from -0.15625 to 0.15625
- sign_offset: int32 [1], replicated, may hold values from 1 to 999999999
Outputs:
- out_plus: bfloat16 [16384, 4096], P(('dp', 'mp'))
- out_minus: bfloat16 [16384, 4096], P(('dp', 'mp'))
Inputs may be any that keep to these rules, and one draw needn't show every extreme that they name: `expert_ids`: within each aligned block of 128 tokens (the tokens of one device) no expert is named by more than 3 routes, a bound that some block reaches.
All inputs are finite; a program needn't handle non-finite values.
Results may differ from a plain program's by a relative error of at most 0.01.
Values may be sent and summed in bfloat16 or wider, within the bound.
A program may use at most 128 MiB of HBM per device.

v0:
```python
import jax
import jax.numpy as jnp
from jax import lax
from jax.sharding import PartitionSpec as P

FF = 1536
epsilon_step = 0.005


def mixing(number):
    number = number ^ lax.shift_right_logical(number, jnp.full_like(number, 16))
    number = number * 73244475
    number = number ^ lax.shift_right_logical(number, jnp.full_like(number, 16))
    number = number * 73244475
    return number ^ lax.shift_right_logical(number, jnp.full_like(number, 16))


def sign_noise(offset_mixed, position, matrix_tag):
    hashed = mixing(position * 3 + matrix_tag ^ offset_mixed)
    parity = lax.shift_right_logical(hashed, jnp.full_like(hashed, 9)) & 1
    return (parity * 2 - 1).astype(jnp.float32)


def perturb(weight, noise, direction):
    return (weight.astype(jnp.float32) + direction * epsilon_step * noise).astype(jnp.bfloat16)


def expert_rows(arrived, weight_sets):
    lead_shape = arrived.shape
    model_width = lead_shape[-1]
    per_expert = []
    for local_expert in range(lead_shape[2]):
        flat_rows = arrived[:, :, local_expert].reshape(-1, model_width)
        by_pass = []
        for gate_moved, up_moved, down_moved in weight_sets[local_expert]:
            gate_act = jnp.dot(flat_rows, gate_moved, preferred_element_type=jnp.float32)
            up_act = jnp.dot(flat_rows, up_moved, preferred_element_type=jnp.float32)
            hidden = (jax.nn.silu(gate_act) * up_act).astype(jnp.bfloat16)
            by_pass.append(
                jnp.dot(hidden, down_moved, preferred_element_type=jnp.float32).astype(jnp.bfloat16)
            )
        stacked = jnp.stack(by_pass, axis=1).reshape(
            lead_shape[0], lead_shape[1], lead_shape[3], len(by_pass), model_width
        )
        per_expert.append(stacked)
    return jnp.stack(per_expert, axis=2)


def shards(tokens, expert_ids, gate_probs, gate_weight, up_weight, down_weight, sign_offset):
    mp_count = lax.axis_size("mp")
    tok_rows, model_width = tokens.shape
    route_count = expert_ids.shape[1]
    local_count = gate_weight.shape[0]
    quarter = gate_weight.shape[2]
    expert_count = local_count * mp_count
    capacity = 3 * tok_rows * route_count // (2 * expert_count)
    offset_mixed = mixing(sign_offset[0] * 668265261 + 12345)
    expert_base = lax.axis_index("mp") * local_count
    hidden_base = lax.axis_index("dp") * quarter
    width_axis = lax.broadcasted_iota(jnp.int32, (model_width, quarter), 0)
    unit_axis = lax.broadcasted_iota(jnp.int32, (model_width, quarter), 1) + hidden_base
    plus_sets = []
    minus_sets = []
    for local_expert in range(local_count):
        expert_global = expert_base + local_expert
        gate_pos = (expert_global * model_width + width_axis) * FF + unit_axis
        down_pos = (expert_global * FF + unit_axis.T) * model_width + width_axis.T
        noise_gate = sign_noise(offset_mixed, gate_pos, 0)
        noise_up = sign_noise(offset_mixed, gate_pos, 1)
        noise_down = sign_noise(offset_mixed, down_pos, 2)
        for direction, target in ((1.0, plus_sets), (-1.0, minus_sets)):
            target.append(
                (
                    perturb(gate_weight[local_expert], noise_gate, direction),
                    perturb(up_weight[local_expert], noise_up, direction),
                    perturb(down_weight[local_expert], noise_down, direction),
                )
            )
    route_flat = expert_ids.reshape(-1)
    expert_axis = lax.broadcasted_iota(jnp.int32, (route_flat.shape[0], expert_count), 1)
    onehot = (route_flat[:, None] == expert_axis).astype(jnp.int32)
    earlier = jnp.cumsum(onehot, axis=0, dtype=jnp.int32) - onehot
    rank_in = jnp.sum(earlier * onehot, axis=1, dtype=jnp.int32)
    slot_of = (route_flat * capacity + rank_in).reshape(tok_rows, route_count)
    slot_axis = lax.broadcasted_iota(jnp.int32, (expert_count * capacity, tok_rows), 0)
    selector = (slot_axis == slot_of[:, 0][None, :]).astype(jnp.float32)
    outgoing = jnp.dot(
        selector.astype(jnp.bfloat16), tokens, preferred_element_type=jnp.float32
    ).astype(jnp.bfloat16)
    outgoing = outgoing.reshape(mp_count, local_count, capacity, model_width)
    grouped = lax.all_gather(outgoing[None], "dp", axis=0, tiled=True)
    arrived = lax.all_to_all(grouped, "mp", split_axis=1, concat_axis=1, tiled=True)

    def finish(weight_sets):
        partials = expert_rows(arrived, weight_sets)
        returned = lax.all_to_all(partials, "mp", split_axis=1, concat_axis=1, tiled=True)
        summed = lax.psum_scatter(
            returned.astype(jnp.float32).astype(jnp.bfloat16), "dp", scatter_dimension=0, tiled=True
        ).astype(jnp.float32)
        return summed[0].astype(jnp.bfloat16)

    def combine(result, pass_index):
        flat_out = result.reshape(expert_count * capacity, result.shape[3], model_width)[
            :, pass_index
        ]
        picked = (
            jnp.take(flat_out, slot_of.reshape(-1), axis=0)
            .reshape(tok_rows, route_count, model_width)
            .astype(jnp.float32)
        )
        return jnp.sum(gate_probs[:, :, None] * picked, axis=1).astype(jnp.bfloat16)

    plus_result = finish([[entry_set] for entry_set in plus_sets])
    minus_result = finish([[entry_set] for entry_set in minus_sets])
    return (combine(plus_result, 0), combine(minus_result, 0))


def solution(mesh):
    in_specs = (
        P(("dp", "mp"), None),
        P(("dp", "mp"), None),
        P(("dp", "mp"), None),
        P("mp", None, "dp"),
        P("mp", None, "dp"),
        P("mp", "dp", None),
        P(),
    )
    out_specs = (P(("dp", "mp"), None), P(("dp", "mp"), None))
    return jax.shard_map(shards, mesh=mesh, in_specs=in_specs, out_specs=out_specs, check_vma=False)
```

profile of v0, /device:TPU:1, one launch (start us, length us, event | category | flops | bytes accessed | tf_op | source)
XLA Modules:
  0.0 660.6 jit_solution(3425733113894375996)
XLA Ops:
  17.6 69.3 %all-gather.2.cloned.1.call-done = bf16[4,32,2,3,4096]{4,1,3,2,0:T(8,128)(2,1)} async-done(((bf16[1,32,2,3,4096]{4,1,3,2,0:T(8,128)(2,1)}), bf16[4,32,2,3,4096]{4,1,3,2,0:T(8,128)(2,1)}) %all-gather.2.cloned.1.call-update) | async-done | bytes 6291472 | tf_op jit(solution)/shard_map/all_gather | solution.py:91
  86.8 10.3 %copy.14 = bf16[4,32,2,3,4096]{4,0,3,2,1:T(4,128)(2,1)} copy(bf16[4,32,2,3,4096]{4,1,3,2,0:T(8,128)(2,1)} %all-gather.2.cloned.1.call-done) | data formatting | bytes 12582912 | tf_op jit(solution)/shard_map/all_gather | solution.py:91
  97.1 7.6 %all-to-all-start = ((bf16[4,32,2,3,4096]{4,0,3,2,1:T(4,128)(2,1)}), bf16[4,32,2,3,4096]{4,0,3,2,1:T(4,128)(2,1)}, u32[]{:S(2)}, u32[]{:S(2)}) async-start(bf16[4,32,2,3,4096]{4,0,3,2,1:T(4,128)(2,1)} %copy.14), calls=%async_computation | async-start | bytes 12582912 | tf_op jit(solution)/shard_map/all_to_all | solution.py:92
  105.7 77.0 %all-to-all-done = bf16[4,32,2,3,4096]{4,0,3,2,1:T(4,128)(2,1)} async-done(((bf16[4,32,2,3,4096]{4,0,3,2,1:T(4,128)(2,1)}), bf16[4,32,2,3,4096]{4,0,3,2,1:T(4,128)(2,1)}, u32[]{:S(2)}, u32[]{:S(2)}) %all-to-all-start) | async-done | bytes 6291488 | tf_op jit(solution)/shard_map/all_to_all | solution.py:92
  182.7 6.9 %fusion.296 = (bf16[4,32,1,3,4096]{4,0,3,2,1:T(4,128)(2,1)}, bf16[4,32,1,3,4096]{4,0,3,2,1:T(4,128)(2,1)S(1)}) fusion(bf16[4,32,2,3,4096]{4,0,3,2,1:T(4,128)(2,1)} %all-to-all-done), kind=kLoop, calls=%fused_computation.284 | loop fusion | bytes 12582912 | tf_op jit(solution)/shard_map/slice | solution.py:33
  189.6 4.6 copy.16
  194.3 7.4 %reshape_squeeze.9 = bf16[384,4096]{1,0:T(8,128)(2,1)} reshape(bf16[4,32,1,3,4096]{4,3,1,0,2:T(4,128)(2,1)} %copy.16) | data formatting | bytes 6291456 | tf_op jit(solution)/shard_map/reshape;squeeze | solution.py:33
  201.7 7.5 %fusion.118 = f32[384,384]{1,0:T(8,128)S(1)} fusion(bf16[384,4096]{1,0:T(8,128)(2,1)} %reshape_squeeze.9, s32[4096]{0:T(1024)S(1)} %add_multiply_fusion.2, s32[]{:T(128)S(6)} %xor.269, s32[384]{0:T(512)S(1)} %iota_add_fusion, bf16[2,4096,384]{2,1,0:T(8,128)(2,1)} %param.12), kind=kOutput, calls=%fused_computation.151 | convolution fusion | flops 1239416832 | bytes 6899204 | tf_op jit(solution)/shard_map/dot_general | solution.py:36
  209.2 15.7 %convolution_convert_fusion.2 = bf16[384,4096]{1,0:T(8,128)(2,1)} fusion(s32[384]{0:T(512)S(1)} %get-tuple-element.9, s32[]{:T(128)S(6)} %xor.269, bf16[2,384,4096]{2,1,0:T(8,128)(2,1)} %param.14, bf16[384,4096]{1,0:T(8,128)(2,1)} %reshape_squeeze.9, s32[4096]{0:T(1024)S(1)} %add_multiply_fusion.2, s32[384]{0:T(512)S(1)} %iota_add_fusion, ...), kind=kOutput, calls=%fused_computation.92 | convolution fusion | flops 2484436992 | bytes 13193216 | tf_op jit(solution)/shard_map/dot_general | solution.py:40
  224.9 7.1 %stack_reshape_stack.13 = bf16[4,32,1,3,1,4096]{5,3,1,0,4,2:T(4,128)(2,1)} reshape(bf16[384,4096]{1,0:T(8,128)(2,1)} %convolution_convert_fusion.2) | data formatting | bytes 6291456 | tf_op jit(solution)/shard_map/stack;reshape;stack | solution.py:46
  232.0 7.4 %copy.15 = bf16[4,32,1,3,4096]{4,3,1,0,2:T(4,128)(2,1)} copy(bf16[4,32,1,3,4096]{4,0,3,2,1:T(4,128)(2,1)} %get-tuple-element.5) | data formatting | bytes 6291456 | tf_op jit(solution)/shard_map/slice | solution.py:33
  239.4 7.4 %reshape_squeeze.8 = bf16[384,4096]{1,0:T(8,128)(2,1)} reshape(bf16[4,32,1,3,4096]{4,3,1,0,2:T(4,128)(2,1)} %copy.15) | data formatting | bytes 6291456 | tf_op jit(solution)/shard_map/reshape;squeeze | solution.py:33
  246.8 7.5 %fusion.110 = f32[384,384]{1,0:T(8,128)S(1)} fusion(bf16[384,4096]{1,0:T(8,128)(2,1)} %reshape_squeeze.8, s32[]{:T(128)S(6)} %xor.269, s32[384]{0:T(512)S(1)} %iota_add_fusion, s32[4096]{0:T(1024)S(1)} %add_multiply_fusion.3, bf16[2,4096,384]{2,1,0:T(8,128)(2,1)} %param.12), kind=kOutput, calls=%fused_computation.147 | convolution fusion | flops 1239416832 | bytes 6899204 | tf_op jit(solution)/shard_map/dot_general | solution.py:36
  254.3 15.5 %convolution_convert_fusion.3 = bf16[384,4096]{1,0:T(8,128)(2,1)} fusion(s32[]{:T(128)S(6)} %xor.269, s32[384]{0:T(512)S(1)} %get-tuple-element.10, bf16[2,384,4096]{2,1,0:T(8,128)(2,1)} %param.14, bf16[384,4096]{1,0:T(8,128)(2,1)} %reshape_squeeze.8, s32[384]{0:T(512)S(1)} %iota_add_fusion, s32[4096]{0:T(1024)S(1)} %add_multiply_fusion.3, ...), kind=kOutput, calls=%fused_computation.93 | convolution fusion | flops 2484436992 | bytes 13193216 | tf_op jit(solution)/shard_map/dot_general | solution.py:40
  269.8 7.1 %stack_reshape_stack.12 = bf16[4,32,1,3,1,4096]{5,3,1,0,4,2:T(4,128)(2,1)} reshape(bf16[384,4096]{1,0:T(8,128)(2,1)} %convolution_convert_fusion.3) | data formatting | bytes 6291456 | tf_op jit(solution)/shard_map/stack;reshape;stack | solution.py:46
  276.9 8.7 %pad_maximum_fusion = bf16[4,32,2,3,1,4096]{5,3,1,0,4,2:T(4,128)(2,1)} fusion(bf16[4,32,1,3,1,4096]{5,3,1,0,4,2:T(4,128)(2,1)} %stack_reshape_stack.13, bf16[4,32,1,3,1,4096]{5,3,1,0,4,2:T(4,128)(2,1)} %stack_reshape_stack.12), kind=kLoop, calls=%fused_computation.20 | loop fusion | flops 3145728 | bytes 12582912 | tf_op jit(solution)/shard_map/stack | solution.py:46
  285.6 21.7 %copy.17 = bf16[4,32,2,3,1,4096]{5,0,4,3,2,1:T(4,128)(2,1)} copy(bf16[4,32,2,3,1,4096]{5,3,1,0,4,2:T(4,128)(2,1)} %pad_maximum_fusion) | data formatting | bytes 12582912 | tf_op jit(solution)/shard_map/stack | solution.py:46
  307.3 87.6 %all_to_all.15 = bf16[4,32,2,3,1,4096]{5,0,4,3,2,1:T(4,128)(2,1)S(1)} all-to-all(bf16[4,32,2,3,1,4096]{5,0,4,3,2,1:T(4,128)(2,1)} %copy.17), channel_id=1, replica_groups=mesh['dp'=4,'mp'=32] {'mp'}, dimensions={1} | all-to-all | bytes 12582912 | tf_op jit(solution)/shard_map/all_to_all | solution.py:96
  394.9 6.1 copy.18
  401.2 7.5 %fusion.120 = f32[384,384]{1,0:T(8,128)S(1)} fusion(bf16[384,4096]{1,0:T(8,128)(2,1)} %reshape_squeeze.9, s32[4096]{0:T(1024)S(1)} %add_multiply_fusion.2, s32[]{:T(128)S(6)} %xor.269, s32[384]{0:T(512)S(1)} %iota_add_fusion, bf16[2,4096,384]{2,1,0:T(8,128)(2,1)} %param.12), kind=kOutput, calls=%fused_computation.152 | convolution fusion | flops 1239416832 | bytes 6899204 | tf_op jit(solution)/shard_map/dot_general | solution.py:36
  408.7 15.5 %convolution_convert_fusion = bf16[384,4096]{1,0:T(8,128)(2,1)} fusion(s32[384]{0:T(512)S(1)} %get-tuple-element.9, s32[]{:T(128)S(6)} %xor.269, bf16[2,384,4096]{2,1,0:T(8,128)(2,1)} %param.14, bf16[384,4096]{1,0:T(8,128)(2,1)} %reshape_squeeze.9, s32[4096]{0:T(1024)S(1)} %add_multiply_fusion.2, s32[384]{0:T(512)S(1)} %iota_add_fusion, ...), kind=kOutput, calls=%fused_computation.90 | convolution fusion | flops 2484436992 | bytes 13193216 | tf_op jit(solution)/shard_map/dot_general | solution.py:40
  424.2 7.1 %stack_reshape_stack.15 = bf16[4,32,1,3,1,4096]{5,3,1,0,4,2:T(4,128)(2,1)} reshape(bf16[384,4096]{1,0:T(8,128)(2,1)} %convolution_convert_fusion) | data formatting | bytes 6291456 | tf_op jit(solution)/shard_map/stack;reshape;stack | solution.py:46
  431.3 7.6 %fusion.112 = f32[384,384]{1,0:T(8,128)S(1)} fusion(bf16[384,4096]{1,0:T(8,128)(2,1)} %reshape_squeeze.8, s32[]{:T(128)S(6)} %xor.269, s32[384]{0:T(512)S(1)} %iota_add_fusion, s32[4096]{0:T(1024)S(1)} %add_multiply_fusion.3, bf16[2,4096,384]{2,1,0:T(8,128)(2,1)} %param.12), kind=kOutput, calls=%fused_computation.148 | convolution fusion | flops 1239416832 | bytes 6899204 | tf_op jit(solution)/shard_map/dot_general | solution.py:36
  438.9 15.9 %convolution_convert_fusion.1 = bf16[384,4096]{1,0:T(8,128)(2,1)} fusion(s32[]{:T(128)S(6)} %xor.269, s32[384]{0:T(512)S(1)} %get-tuple-element.10, bf16[2,384,4096]{2,1,0:T(8,128)(2,1)} %param.14, bf16[384,4096]{1,0:T(8,128)(2,1)} %reshape_squeeze.8, s32[384]{0:T(512)S(1)} %iota_add_fusion, s32[4096]{0:T(1024)S(1)} %add_multiply_fusion.3, ...), kind=kOutput, calls=%fused_computation.91 | convolution fusion | flops 2484436992 | bytes 13193216 | tf_op jit(solution)/shard_map/dot_general | solution.py:40
  454.8 7.1 %stack_reshape_stack.14 = bf16[4,32,1,3,1,4096]{5,3,1,0,4,2:T(4,128)(2,1)} reshape(bf16[384,4096]{1,0:T(8,128)(2,1)} %convolution_convert_fusion.1) | data formatting | bytes 6291456 | tf_op jit(solution)/shard_map/stack;reshape;stack | solution.py:46
  461.9 8.8 %pad_maximum_fusion.1 = bf16[4,32,2,3,1,4096]{5,3,1,0,4,2:T(4,128)(2,1)} fusion(bf16[4,32,1,3,1,4096]{5,3,1,0,4,2:T(4,128)(2,1)} %stack_reshape_stack.15, bf16[4,32,1,3,1,4096]{5,3,1,0,4,2:T(4,128)(2,1)} %stack_reshape_stack.14), kind=kLoop, calls=%fused_computation.21 | loop fusion | flops 3145728 | bytes 12582912 | tf_op jit(solution)/shard_map/stack | solution.py:46
  470.6 21.3 %copy.20 = bf16[4,32,2,3,1,4096]{5,0,4,3,2,1:T(4,128)(2,1)} copy(bf16[4,32,2,3,1,4096]{5,3,1,0,4,2:T(4,128)(2,1)} %pad_maximum_fusion.1) | data formatting | bytes 12582912 | tf_op jit(solution)/shard_map/stack | solution.py:46
  492.0 78.0 %all_to_all.16 = bf16[4,32,2,3,1,4096]{5,0,4,3,2,1:T(4,128)(2,1)S(1)} all-to-all(bf16[4,32,2,3,1,4096]{5,0,4,3,2,1:T(4,128)(2,1)} %copy.20), channel_id=1, replica_groups=mesh['dp'=4,'mp'=32] {'mp'}, dimensions={1} | all-to-all | bytes 12582912 | tf_op jit(solution)/shard_map/all_to_all | solution.py:96
  569.9 6.1 copy.21
  576.7 4.1 copy.19
  584.1 53.3 %reduce-scatter.5.cloned.1.call-done = bf16[1,32,2,3,1,4096]{5,1,4,3,2,0:T(8,128)(2,1)} async-done(((bf16[4,32,2,3,1,4096]{5,1,4,3,2,0:T(8,128)(2,1)}), bf16[1,32,2,3,1,4096]{5,1,4,3,2,0:T(8,128)(2,1)}) %reduce-scatter.5.cloned.1.call-update) | async-done | bytes 1572880 | tf_op jit(solution)/shard_map/reduce_scatter | solution.py:97
  641.5 4.3 convert_element_type.279
  (39 shorter events, 26.7 us)
Async XLA Ops:
  7.2 3.6 copy-start
  7.2 79.6 %all-gather.2.cloned.1.call-start = ((), (), s32[]{:S(2)}) async-start(), calls=%async_computation.5 | async-start | bytes 7864320 | tf_op jit(solution)/shard_map/all_gather | solution.py:91
  10.2 0.5 copy-start.4
  97.1 85.6 %all-to-all-start = ((bf16[4,32,2,3,4096]{4,0,3,2,1:T(4,128)(2,1)}), bf16[4,32,2,3,4096]{4,0,3,2,1:T(4,128)(2,1)}, u32[]{:S(2)}, u32[]{:S(2)}) async-start(bf16[4,32,2,3,4096]{4,0,3,2,1:T(4,128)(2,1)} %copy.14), calls=%async_computation | async-start | bytes 12582912 | tf_op jit(solution)/shard_map/all_to_all | solution.py:92
  104.7 471.9 %reduce-scatter.3.cloned.1.call-start = ((), (), s32[]{:S(2)}) async-start(), calls=%async_computation.6 | async-start | bytes 7864320 | tf_op jit(solution)/shard_map/reduce_scatter | solution.py:97
  401.1 236.3 %reduce-scatter.5.cloned.1.call-start = ((), (), s32[]{:S(2)}) async-start(), calls=%async_computation.7 | async-start | bytes 7864320 | tf_op jit(solution)/shard_map/reduce_scatter | solution.py:97
  576.0 0.6 copy-start.5
  645.8 8.0 %copy-start.1 = (bf16[128,4096]{1,0:T(8,128)(2,1)S(1)}, bf16[128,4096]{1,0:T(8,128)(2,1)}, u32[]{:S(2)}) copy-start(bf16[128,4096]{1,0:T(8,128)(2,1)} %param.9) | copy-start | bytes 3145732
  648.0 3.9 copy-start.2
  648.0 3.9 copy-start.3
  648.0 3.9 copy-start.6
Sparse Core Ops, SparseCore 0:
  17.7 69.0 all-gather.1
  401.2 61.1 reduce-scatter.2
  576.2 61.2 reduce-scatter.4
where the time goes:
time: 668 us; the launch traced here: 661 us
  waiting for transfers between devices  200 us (30%)
  blocking collectives  166 us (25%)
  local copies, waits for them, and re-layouts  156 us (23%)
  matrix products  94.5 us (14%)
  other arithmetic  22.4 us (3%)
  between operations  14.8 us (2%)
  starting transfers between devices  7.92 us (1%)
    all_to_all x2, blocking collectives, finish(): lax.all_to_all(partials, 'mp', split_axis=1, concat_axis=1, tiled=True)  166 us
    all_to_all x1, waiting for transfers between devices, shards(): lax.all_to_all(grouped, 'mp', split_axis=1, concat_axis=1, tiled=True)  77 us
    another operation x6, local copies, waits for them, and re-layouts, expert_rows(): return jnp.stack(per_expert, axis=2)  71.4 us
    all_gather x1, waiting for transfers between devices, shards(): grouped = lax.all_gather(outgoing[None], 'dp', axis=0, tiled=True)  69.3 us
    dot_general x4, matrix products, expert_rows(): jnp.dot(hidden, down_moved, preferred_element_type=jnp.float32)  62.6 us
    reduce_scatter x2, waiting for transfers between devices, finish(): lax.psum_scatter(returned.astype(jnp.float32).astype(jnp.bfloat16), 'dp',...  53.4 us
    dot_general x4, matrix products, expert_rows(): jnp.dot(flat_rows, gate_moved, preferred_element_type=jnp.float32)  30.1 us
    slice x3, local copies, waits for them, and re-layouts, expert_rows(): flat_rows = arrived[:, :, local_expert].reshape(-1, model_width)  19 us
  transfers between devices with their start and end apart: 4, of which 3 were waited for; matrix products, arithmetic and copies ran while one was open for 16% of the time, Pallas kernels for 0%

commit v1 on v0

--- a/solution.py
+++ b/solution.py
@@ -93,7 +93,10 @@
 
     def finish(weight_sets):
         partials = expert_rows(arrived, weight_sets)
-        returned = lax.all_to_all(partials, "mp", split_axis=1, concat_axis=1, tiled=True)
+        size = lax.axis_size("mp")
+        blocks = jnp.stack(jnp.split(partials, size, axis=1), axis=0)
+        blocks = lax.all_to_all(blocks, "mp", split_axis=0, concat_axis=0)
+        returned = jnp.concatenate(blocks, axis=1)
         summed = lax.psum_scatter(
             returned.astype(jnp.float32).astype(jnp.bfloat16), "dp", scatter_dimension=0, tiled=True
         ).astype(jnp.float32)

time: 668 us -> 676 us (1.012)
  blocking collectives: 166 us -> 87.9 us
  local copies, waits for them, and re-layouts: 156 us -> 232 us
  starting transfers between devices: 7.92 us -> 33.2 us
  other arithmetic: 22.4 us -> 5.04 us
    all_to_all x2 -> x1, blocking collectives: 166 us -> 87.9 us  [finish(): blocks = lax.all_to_all(blocks, 'mp', split_axis=0, concat_axis=0)]
    unnamed x14 -> x102, local copies, waits for them, and re-layouts: 1.15 us -> 67.9 us
    another operation x0 -> x4, local copies, waits for them, and re-layouts: none -> 46.2 us  [finish(): blocks = jnp.stack(jnp.split(partials, size, axis=1), axis=0)]
    another operation x6, local copies, waits for them, and re-layouts: 71.4 us -> 34.1 us  [expert_rows(): return jnp.stack(per_expert, axis=2)]
    another operation x2 -> x0, other arithmetic: 17.5 us -> none  [expert_rows(): return jnp.stack(per_expert, axis=2)]
    reshape x0 -> x2, local copies, waits for them, and re-layouts: none -> 14.9 us  [finish(): returned = jnp.concatenate(blocks, axis=1)]
    all_to_all x0 -> x1, starting transfers between devices: none -> 13.7 us  [finish(): blocks = lax.all_to_all(blocks, 'mp', split_axis=0, concat_axis=0)]
    all_to_all x2 -> x0, local copies, waits for them, and re-layouts: 12.2 us -> none  [finish(): lax.all_to_all(partials, 'mp', split_axis=1, concat_axis=1, tiled=True)]
  transfers between devices with their start and end apart: 4 -> 5, of which waited for: 3 -> 4; matrix products, arithmetic and copies ran while one was open for 16% -> 18% of each run, Pallas kernels for 0% -> 0%
where the time goes in v1:
time: 676 us; the launch traced here: 668 us
  local copies, waits for them, and re-layouts  232 us (34%)
  waiting for transfers between devices  204 us (30%)
  matrix products  91.1 us (13%)
  blocking collectives  87.9 us (13%)
  starting transfers between devices  33.2 us (5%)
  between operations  15 us (2%)
    all_to_all x1, blocking collectives, finish(): blocks = lax.all_to_all(blocks, 'mp', split_axis=0, concat_axis=0)  87.9 us
    all_to_all x1, waiting for transfers between devices, shards(): lax.all_to_all(grouped, 'mp', split_axis=1, concat_axis=1, tiled=True)  76.7 us
    all_gather x1, waiting for transfers between devices, shards(): grouped = lax.all_gather(outgoing[None], 'dp', axis=0, tiled=True)  69.2 us
    unnamed x102, local copies, waits for them, and re-layouts  67.9 us
    dot_general x4, matrix products, expert_rows(): jnp.dot(hidden, down_moved, preferred_element_type=jnp.float32)  62.1 us
    reduce_scatter x2, waiting for transfers between devices, finish(): lax.psum_scatter(returned.astype(jnp.float32).astype(jnp.bfloat16), 'dp',...  53.2 us
    another operation x4, local copies, waits for them, and re-layouts, finish(): blocks = jnp.stack(jnp.split(partials, size, axis=1), axis=0)  46.2 us
    another operation x6, local copies, waits for them, and re-layouts, expert_rows(): return jnp.stack(per_expert, axis=2)  34.1 us
  transfers between devices with their start and end apart: 5, of which 4 were waited for; matrix products, arithmetic and copies ran while one was open for 18% of the time, Pallas kernels for 0%

profile of v1, /device:TPU:1, one launch (start us, length us, event | category | flops | bytes accessed | tf_op | source)
XLA Modules:
  0.0 668.2 jit_solution(3650965405681382184)
XLA Ops:
  17.7 69.2 %all-gather.2.cloned.1.call-done = bf16[4,32,2,3,4096]{4,1,3,2,0:T(8,128)(2,1)} async-done(((bf16[1,32,2,3,4096]{4,1,3,2,0:T(8,128)(2,1)}), bf16[4,32,2,3,4096]{4,1,3,2,0:T(8,128)(2,1)}) %all-gather.2.cloned.1.call-update) | async-done | bytes 6291472 | tf_op jit(solution)/shard_map/all_gather | solution.py:91
  86.9 10.2 %copy.134 = bf16[4,32,2,3,4096]{4,0,3,2,1:T(4,128)(2,1)} copy(bf16[4,32,2,3,4096]{4,1,3,2,0:T(8,128)(2,1)} %all-gather.2.cloned.1.call-done) | data formatting | bytes 12582912 | tf_op jit(solution)/shard_map/all_gather | solution.py:91
  97.2 19.0 %all-to-all-start = ((bf16[4,32,2,3,4096]{4,0,3,2,1:T(4,128)(2,1)}), bf16[4,32,2,3,4096]{4,0,3,2,1:T(4,128)(2,1)}, u32[]{:S(2)}, u32[]{:S(2)}) async-start(bf16[4,32,2,3,4096]{4,0,3,2,1:T(4,128)(2,1)} %copy.134), calls=%async_computation | async-start | bytes 12582912 | tf_op jit(solution)/shard_map/all_to_all | solution.py:92
  116.9 76.7 %all-to-all-done = bf16[4,32,2,3,4096]{4,0,3,2,1:T(4,128)(2,1)} async-done(((bf16[4,32,2,3,4096]{4,0,3,2,1:T(4,128)(2,1)}), bf16[4,32,2,3,4096]{4,0,3,2,1:T(4,128)(2,1)}, u32[]{:S(2)}, u32[]{:S(2)}) %all-to-all-start) | async-done | bytes 6291488 | tf_op jit(solution)/shard_map/all_to_all | solution.py:92
  193.6 7.0 %fusion.360 = (bf16[4,32,1,3,4096]{4,0,3,2,1:T(4,128)(2,1)S(1)}, bf16[4,32,1,3,4096]{4,0,3,2,1:T(4,128)(2,1)}) fusion(bf16[4,32,2,3,4096]{4,0,3,2,1:T(4,128)(2,1)} %all-to-all-done), kind=kLoop, calls=%fused_computation.414 | loop fusion | bytes 12582912 | tf_op jit(solution)/shard_map/slice | solution.py:33
  200.5 4.8 copy.136
  205.3 7.5 %reshape_squeeze.9 = bf16[384,4096]{1,0:T(8,128)(2,1)} reshape(bf16[4,32,1,3,4096]{4,3,1,0,2:T(4,128)(2,1)} %copy.136) | data formatting | bytes 6291456 | tf_op jit(solution)/shard_map/reshape;squeeze | solution.py:33
  212.9 8.5 %fusion.118 = f32[384,384]{1,0:T(8,128)} fusion(bf16[384,4096]{1,0:T(8,128)(2,1)} %reshape_squeeze.9, s32[4096]{0:T(1024)S(1)} %add_multiply_fusion.2, s32[]{:T(128)S(6)} %xor.269, s32[384]{0:T(512)S(1)} %iota_add_fusion, bf16[2,4096,384]{2,1,0:T(8,128)(2,1)} %param.12), kind=kOutput, calls=%fused_computation.149 | convolution fusion | flops 1239416832 | bytes 6899204 | tf_op jit(solution)/shard_map/dot_general | solution.py:36
  221.3 5.5 fusion.120
  226.9 4.8 copy.135
  231.7 7.7 %reshape_squeeze.8 = bf16[384,4096]{1,0:T(8,128)(2,1)} reshape(bf16[4,32,1,3,4096]{4,3,1,0,2:T(4,128)(2,1)} %copy.135) | data formatting | bytes 6291456 | tf_op jit(solution)/shard_map/reshape;squeeze | solution.py:33
  239.4 8.5 %fusion.110 = f32[384,384]{1,0:T(8,128)} fusion(bf16[384,4096]{1,0:T(8,128)(2,1)} %reshape_squeeze.8, s32[]{:T(128)S(6)} %xor.269, s32[384]{0:T(512)S(1)} %iota_add_fusion, s32[4096]{0:T(1024)S(1)} %add_multiply_fusion.3, bf16[2,4096,384]{2,1,0:T(8,128)(2,1)} %param.12), kind=kOutput, calls=%fused_computation.145 | convolution fusion | flops 1239416832 | bytes 6899204 | tf_op jit(solution)/shard_map/dot_general | solution.py:36
  247.9 4.8 fusion.112
  252.7 16.0 %convolution_convert_fusion.2 = bf16[384,4096]{1,0:T(8,128)(2,1)} fusion(s32[384]{0:T(512)S(1)} %get-tuple-element.9, s32[]{:T(128)S(6)} %xor.269, bf16[2,384,4096]{2,1,0:T(8,128)(2,1)} %param.14, bf16[384,4096]{1,0:T(8,128)(2,1)} %reshape_squeeze.9, s32[4096]{0:T(1024)S(1)} %add_multiply_fusion.2, s32[384]{0:T(512)S(1)} %iota_add_fusion, ...), kind=kOutput, calls=%fused_computation.90 | convolution fusion | flops 2484436992 | bytes 13193216 | tf_op jit(solution)/shard_map/dot_general | solution.py:40
  268.7 7.4 %stack_reshape_stack.13 = bf16[4,32,1,3,1,4096]{5,3,1,0,4,2:T(4,128)(2,1)} reshape(bf16[384,4096]{1,0:T(8,128)(2,1)} %convolution_convert_fusion.2) | data formatting | bytes 6291456 | tf_op jit(solution)/shard_map/stack;reshape;stack | solution.py:46
  276.1 15.3 %convolution_convert_fusion.3 = bf16[384,4096]{1,0:T(8,128)(2,1)} fusion(s32[]{:T(128)S(6)} %xor.269, s32[384]{0:T(512)S(1)} %get-tuple-element.10, bf16[2,384,4096]{2,1,0:T(8,128)(2,1)} %param.14, bf16[384,4096]{1,0:T(8,128)(2,1)} %reshape_squeeze.8, s32[384]{0:T(512)S(1)} %iota_add_fusion, s32[4096]{0:T(1024)S(1)} %add_multiply_fusion.3, ...), kind=kOutput, calls=%fused_computation.91 | convolution fusion | flops 2484436992 | bytes 13193216 | tf_op jit(solution)/shard_map/dot_general | solution.py:40
  291.4 7.3 %stack_reshape_stack.12 = bf16[4,32,1,3,1,4096]{5,3,1,0,4,2:T(4,128)(2,1)} reshape(bf16[384,4096]{1,0:T(8,128)(2,1)} %convolution_convert_fusion.3) | data formatting | bytes 6291456 | tf_op jit(solution)/shard_map/stack;reshape;stack | solution.py:46
  298.8 4.3 constant_dynamic-update-slice_fusion.1
  331.4 21.6 %copy.168 = bf16[32,4,1,2,3,1,4096]{6,1,5,4,3,2,0:T(4,128)(2,1)} copy(bf16[32,4,1,2,3,1,4096]{6,4,1,3,5,2,0:T(4,128)(2,1)} %fusion.226) | data formatting | bytes 12582912 | tf_op jit(solution)/shard_map/stack | solution.py:97
  353.0 13.7 %all-to-all-start.1 = ((bf16[32,4,1,2,3,1,4096]{6,1,5,4,3,2,0:T(4,128)(2,1)}), bf16[32,4,1,2,3,1,4096]{6,1,5,4,3,2,0:T(4,128)(2,1)}, u32[]{:S(2)}, u32[]{:S(2)}) async-start(bf16[32,4,1,2,3,1,4096]{6,1,5,4,3,2,0:T(4,128)(2,1)} %copy.168), calls=%async_computation.1 | async-start | bytes 12582912 | tf_op jit(solution)/shard_map/all_to_all | solution.py:98
  366.9 15.4 %convolution_convert_fusion = bf16[384,4096]{1,0:T(8,128)(2,1)} fusion(s32[384]{0:T(512)S(1)} %get-tuple-element.9, s32[]{:T(128)S(6)} %xor.269, bf16[2,384,4096]{2,1,0:T(8,128)(2,1)} %param.14, bf16[384,4096]{1,0:T(8,128)(2,1)} %reshape_squeeze.9, s32[4096]{0:T(1024)S(1)} %add_multiply_fusion.2, s32[384]{0:T(512)S(1)} %iota_add_fusion, ...), kind=kOutput, calls=%fused_computation.88 | convolution fusion | flops 2484436992 | bytes 13193216 | tf_op jit(solution)/shard_map/dot_general | solution.py:40
  382.4 7.4 %stack_reshape_stack.15 = bf16[4,32,1,3,1,4096]{5,3,1,0,4,2:T(4,128)(2,1)} reshape(bf16[384,4096]{1,0:T(8,128)(2,1)} %convolution_convert_fusion) | data formatting | bytes 6291456 | tf_op jit(solution)/shard_map/stack;reshape;stack | solution.py:46
  389.7 15.3 %convolution_convert_fusion.1 = bf16[384,4096]{1,0:T(8,128)(2,1)} fusion(s32[]{:T(128)S(6)} %xor.269, s32[384]{0:T(512)S(1)} %get-tuple-element.10, bf16[2,384,4096]{2,1,0:T(8,128)(2,1)} %param.14, bf16[384,4096]{1,0:T(8,128)(2,1)} %reshape_squeeze.8, s32[384]{0:T(512)S(1)} %iota_add_fusion, s32[4096]{0:T(1024)S(1)} %add_multiply_fusion.3, ...), kind=kOutput, calls=%fused_computation.89 | convolution fusion | flops 2484436992 | bytes 13193216 | tf_op jit(solution)/shard_map/dot_general | solution.py:40
  405.0 7.5 %stack_reshape_stack.14 = bf16[4,32,1,3,1,4096]{5,3,1,0,4,2:T(4,128)(2,1)} reshape(bf16[384,4096]{1,0:T(8,128)(2,1)} %convolution_convert_fusion.1) | data formatting | bytes 6291456 | tf_op jit(solution)/shard_map/stack;reshape;stack | solution.py:46
  412.6 4.3 constant_dynamic-update-slice_fusion.3
  439.8 4.9 all-to-all-done.1
  444.7 8.9 %copy.169 = bf16[4,32,2,3,1,4096]{5,1,4,3,2,0:T(8,128)(2,1)} copy(bf16[4,32,2,3,1,4096]{5,0,3,2,1,4:T(4,128)(2,1)} %bitcast.42) | data formatting | bytes 12582912 | tf_op jit(solution)/shard_map/reshape | solution.py:99
  467.8 22.0 %copy.202 = bf16[32,4,1,2,3,1,4096]{6,1,5,4,3,2,0:T(4,128)(2,1)} copy(bf16[32,4,1,2,3,1,4096]{6,4,1,3,5,2,0:T(4,128)(2,1)} %fusion.194) | data formatting | bytes 12582912 | tf_op jit(solution)/shard_map/stack | solution.py:97
  489.8 87.9 %all_to_all.15 = bf16[32,4,1,2,3,1,4096]{6,1,5,4,3,2,0:T(4,128)(2,1)S(1)} all-to-all(bf16[32,4,1,2,3,1,4096]{6,1,5,4,3,2,0:T(4,128)(2,1)} %copy.202), channel_id=1, replica_groups=mesh['dp'=4,'mp'=32] {'mp'}, dimensions={0} | all-to-all | bytes 12582912 | tf_op jit(solution)/shard_map/all_to_all | solution.py:98
  577.7 6.1 copy.203
  591.9 53.2 %reduce-scatter.5.cloned.1.call-done = bf16[1,32,2,3,1,4096]{5,1,4,3,2,0:T(8,128)(2,1)} async-done(((bf16[4,32,2,3,1,4096]{5,1,4,3,2,0:T(8,128)(2,1)}), bf16[1,32,2,3,1,4096]{5,1,4,3,2,0:T(8,128)(2,1)}) %reduce-scatter.5.cloned.1.call-update) | async-done | bytes 1572880 | tf_op jit(solution)/shard_map/reduce_scatter | solution.py:100
  649.1 4.3 convert_element_type.279
  (132 shorter events, 96.3 us)
Async XLA Ops:
  7.2 3.7 copy-start
  7.2 79.7 %all-gather.2.cloned.1.call-start = ((), (), s32[]{:S(2)}) async-start(), calls=%async_computation.5 | async-start | bytes 7864320 | tf_op jit(solution)/shard_map/all_gather | solution.py:91
  10.3 0.5 copy-start.10
  97.2 96.4 %all-to-all-start = ((bf16[4,32,2,3,4096]{4,0,3,2,1:T(4,128)(2,1)}), bf16[4,32,2,3,4096]{4,0,3,2,1:T(4,128)(2,1)}, u32[]{:S(2)}, u32[]{:S(2)}) async-start(bf16[4,32,2,3,4096]{4,0,3,2,1:T(4,128)(2,1)} %copy.134), calls=%async_computation | async-start | bytes 12582912 | tf_op jit(solution)/shard_map/all_to_all | solution.py:92
  205.3 16.0 %slice-start = ((s8[6291456]{0:T(1024)(128)(4,1)}), s8[2097152]{0:T(1024)(128)(4,1)S(1)}, s32[]{:S(2)}) async-start(s8[6291456]{0:T(1024)(128)(4,1)} %bitcast.480), calls=%async_computation.8 | async-start | bytes 4194304
  212.8 8.5 %copy-start.8 = (bf16[384,4096]{1,0:T(8,128)(2,1)S(1)}, bf16[384,4096]{1,0:T(8,128)(2,1)}, u32[]{:S(2)}) copy-start(bf16[384,4096]{1,0:T(8,128)(2,1)} %reshape_squeeze.9) | copy-start | bytes 9437188
  212.8 8.5 %slice-start.1 = ((s8[6291456]{0:T(1024)(128)(4,1)}), s8[4194304]{0:T(1024)(128)(4,1)S(1)}, s32[]{:S(2)}) async-start(s8[6291456]{0:T(1024)(128)(4,1)} %bitcast.480), calls=%async_computation.9 | async-start | bytes 8388608
  221.3 5.5 copy-start.5
  231.7 16.2 %slice-start.2 = ((s8[6291456]{0:T(1024)(128)(4,1)}), s8[2097152]{0:T(1024)(128)(4,1)S(1)}, s32[]{:S(2)}) async-start(s8[6291456]{0:T(1024)(128)(4,1)} %bitcast.482), calls=%async_computation.10 | async-start | bytes 4194304
  239.4 8.5 %copy-start.7 = (bf16[384,4096]{1,0:T(8,128)(2,1)S(1)}, bf16[384,4096]{1,0:T(8,128)(2,1)}, u32[]{:S(2)}) copy-start(bf16[384,4096]{1,0:T(8,128)(2,1)} %reshape_squeeze.8) | copy-start | bytes 9437188
  239.4 8.5 %slice-start.3 = ((s8[6291456]{0:T(1024)(128)(4,1)}), s8[4194304]{0:T(1024)(128)(4,1)S(1)}, s32[]{:S(2)}) async-start(s8[6291456]{0:T(1024)(128)(4,1)} %bitcast.482), calls=%async_computation.11 | async-start | bytes 8388608
  268.7 7.4 %copy-start.14 = (f32[384,384]{1,0:T(8,128)S(1)}, f32[384,384]{1,0:T(8,128)}, u32[]{:S(2)}) copy-start(f32[384,384]{1,0:T(8,128)} %fusion.110) | copy-start | bytes 1769476
  298.7 4.3 copy-start.4
  353.0 13.9 %copy-start.13 = (f32[384,384]{1,0:T(8,128)S(1)}, f32[384,384]{1,0:T(8,128)}, u32[]{:S(2)}) copy-start(f32[384,384]{1,0:T(8,128)} %fusion.120) | copy-start | bytes 1769476
  353.0 91.6 %all-to-all-start.1 = ((bf16[32,4,1,2,3,1,4096]{6,1,5,4,3,2,0:T(4,128)(2,1)}), bf16[32,4,1,2,3,1,4096]{6,1,5,4,3,2,0:T(4,128)(2,1)}, u32[]{:S(2)}, u32[]{:S(2)}) async-start(bf16[32,4,1,2,3,1,4096]{6,1,5,4,3,2,0:T(4,128)(2,1)} %copy.168), calls=%async_computation.1 | async-start | bytes 12582912 | tf_op jit(solution)/shard_map/all_to_all | solution.py:98
  366.7 217.7 %reduce-scatter.3.cloned.1.call-start = ((), (), s32[]{:S(2)}) async-start(), calls=%async_computation.6 | async-start | bytes 7864320 | tf_op jit(solution)/shard_map/reduce_scatter | solution.py:100
  412.6 4.3 copy-start.3
  419.2 19.8 %copy-start.2 = (bf16[4,32,2,3,1,4096]{5,3,1,0,4,2:T(4,128)(2,1)}, bf16[4,32,2,3,1,4096]{5,3,1,0,4,2:T(4,128)(2,1)S(1)}, u32[]{:S(2)}) copy-start(bf16[4,32,2,3,1,4096]{5,3,1,0,4,2:T(4,128)(2,1)S(1)} %constant_dynamic-update-slice_fusion.2) | copy-start | bytes 18874372
  453.5 191.5 %reduce-scatter.5.cloned.1.call-start = ((), (), s32[]{:S(2)}) async-start(), calls=%async_computation.7 | async-start | bytes 7864320 | tf_op jit(solution)/shard_map/reduce_scatter | solution.py:100
  583.7 0.6 copy-start.11
  653.4 8.0 %copy-start.1 = (bf16[128,4096]{1,0:T(8,128)(2,1)S(1)}, bf16[128,4096]{1,0:T(8,128)(2,1)}, u32[]{:S(2)}) copy-start(bf16[128,4096]{1,0:T(8,128)(2,1)} %param.9) | copy-start | bytes 3145732
  655.6 3.9 copy-start.6
  655.6 3.9 copy-start.9
  655.6 3.9 copy-start.12
Sparse Core Ops, SparseCore 0:
  17.8 69.0 all-gather.1
  453.7 72.2 reduce-scatter.2
  583.9 61.0 reduce-scatter.4
